TPU v7x, 32 devices: a whole 2x2x4 slice. The times are simulated.
32 devices in a mesh: section: 2 (over x), tensor: 4 (over y, core), dp: 4 (over z).
Axes of the slice: x: 2, y: 2, z: 4, core: 2. Of those that a mesh axis runs over, the one named last changes fastest.
Arguments:
- target_ids: int32 [4, 512], P(None, 'section'), may hold values from 0 to 32127
- embed_table: bfloat16 [32128, 4096], P('dp', 'tensor'), may hold values from -16 to 16
- encoder_out: bfloat16 [4, 512, 4096], P('dp', 'section', 'tensor'), may hold values from -32 to 32
- w_query: bfloat16 [4096, 4096], P(('section', 'dp'), 'tensor'), may hold values from -1 to 1
- w_key: bfloat16 [4096, 4096], P(('section', 'dp'), 'tensor'), may hold values from -1 to 1
- w_value: bfloat16 [4096, 4096], P(('section', 'dp'), 'tensor'), may hold values from -0.09375 to 0.09375
Outputs:
- attended: bfloat16 [4, 512, 4096], P('dp', 'section', 'tensor')
All inputs are finite; a program needn't handle non-finite values.
Results may differ from a plain program's by a relative error of at most 0.0096.
Values may be sent and summed in bfloat16 or wider, within the bound.
A program may use at most 128 MiB of HBM per device.

v0:
```python
import jax
import jax.numpy as jnp
from jax import lax
from jax.sharding import PartitionSpec as P

HD = 256


def contract(segment, weight):
    return jnp.dot(segment, weight, preferred_element_type=jnp.float32)


def on_device(target_ids, embed_table, encoder_out, w_query, w_key, w_value):
    table_rows = embed_table.shape[0]
    offset_ids = target_ids - lax.axis_index("dp") * table_rows
    inside = (offset_ids >= 0) & (offset_ids < table_rows)
    picked = jnp.take(embed_table, jnp.clip(offset_ids, 0, table_rows - 1), axis=0)
    partial_rows = jnp.where(inside[..., None], picked.astype(jnp.float32), 0.0)
    decoder_in = lax.psum_scatter(
        partial_rows.astype(jnp.bfloat16), "dp", scatter_dimension=0, tiled=True
    )
    query_weight, key_weight, value_weight = (
        lax.all_gather(w_query, ("section", "dp"), axis=0, tiled=True),
        lax.all_gather(w_key, ("section", "dp"), axis=0, tiled=True),
        lax.all_gather(w_value, ("section", "dp"), axis=0, tiled=True),
    )
    positions = encoder_out.shape[1]
    columns = query_weight.shape[1]
    heads_here = columns // HD
    decoder_rows = decoder_in[0]
    memory_rows = encoder_out[0]
    segment = lax.all_gather(memory_rows, "tensor", axis=1, tiled=True)
    key_sum = contract(segment, key_weight)
    value_sum = contract(segment, value_weight)
    query_sum = contract(lax.all_gather(decoder_rows, "tensor", axis=1, tiled=True), query_weight)
    queries = query_sum.astype(jnp.bfloat16)
    keys_local = key_sum.astype(jnp.bfloat16)
    values_local = value_sum.astype(jnp.bfloat16)
    logit_scale_factor = HD ** (-0.5)
    query_heads = queries.reshape(positions, heads_here, HD)
    segment = (
        lax.all_gather(keys_local, "section", axis=0, tiled=True),
        lax.all_gather(values_local, "section", axis=0, tiled=True),
    )
    peak_now = jnp.full((heads_here, positions), -1e30, jnp.float32)
    key_block = segment[0].reshape(-1, heads_here, HD)
    value_block = segment[1].reshape(-1, heads_here, HD)
    attention_logits = (
        jnp.einsum("phd,nhd->hpn", query_heads, key_block, preferred_element_type=jnp.float32)
        * logit_scale_factor
    )
    new_peak = jnp.maximum(peak_now, jnp.max(attention_logits, axis=-1))
    weights = jnp.exp(attention_logits - new_peak[..., None])
    weight_sum = jnp.sum(weights, axis=-1)
    reduced_precision_weights = weights.astype(jnp.bfloat16)
    weighted_value_total = jnp.einsum(
        "hpn,nhd->hpd", reduced_precision_weights, value_block, preferred_element_type=jnp.float32
    )
    peak_now, weight_sum, weighted_value_total = (new_peak, weight_sum, weighted_value_total)
    result = jnp.transpose(weighted_value_total / weight_sum[..., None], (1, 0, 2))
    return result.reshape(positions, columns).astype(jnp.bfloat16)[None]


def solution(mesh):
    in_specs = (
        P(None, "section"),
        P("dp", "tensor"),
        P("dp", "section", "tensor"),
        P(("section", "dp"), "tensor"),
        P(("section", "dp"), "tensor"),
        P(("section", "dp"), "tensor"),
    )
    out_specs = P("dp", "section", "tensor")
    return jax.shard_map(
        on_device, mesh=mesh, in_specs=in_specs, out_specs=out_specs, check_vma=False
    )
```

profile of v0, /device:TPU:12, one launch (start us, length us, event | category | flops | bytes accessed | tf_op | source)
XLA Modules:
  0.0 509.7 jit_solution(3520769389923749896)
XLA Ops:
  7.4 0.0 reduce-scatter.2.cloned.1.call-start
  7.4 0.7 compare_and_fusion.1
  8.1 0.7 fusion.27
  8.8 12.8 %gather_fusion = bf16[1024,1024]{1,0:T(8,128)(2,1)S(1)} fusion(bf16[8032,1024]{1,0:T(8,128)(2,1)} %param.7, s32[1024]{0:T(1024)S(1)} %broadcast_clamp_fusion), kind=kCustom, calls=%fused_computation | custom fusion | bytes 4198400 | tf_op jit(solution)/shard_map/jit(_take)/gather | solution.py:17
  21.6 1.7 select_convert_fusion
  23.3 0.0 reduce-scatter.2.cloned.1.call-update
  23.3 0.0 all-gather.22.cloned.1.call-start
  23.4 0.5 all-gather.22.cloned.1.call-update
  23.9 0.0 all-gather.12.cloned.1.call-start
  23.9 0.5 all-gather.12.cloned.1.call-update
  24.5 0.0 all-gather.16.cloned.1.call-start
  24.5 0.5 all-gather.16.cloned.1.call-update
  25.1 0.0 all-gather.20.cloned.1.call-start
  25.1 42.5 %reduce-scatter.2.cloned.1.call-done = bf16[1,256,1024]{2,1,0:T(8,128)(2,1)} async-done(((bf16[4,256,1024]{2,1,0:T(8,128)(2,1)}), bf16[1,256,1024]{2,1,0:T(8,128)(2,1)}) %reduce-scatter.2.cloned.1.call-update) | async-done | bytes 524304 | tf_op jit(solution)/shard_map/reduce_scatter | solution.py:19
  67.6 0.0 all-gather.20.cloned.1.call-update
  67.6 0.0 all-gather.10.cloned.1.call-start
  67.6 0.7 all-gather.10.cloned.1.call-update
  68.4 0.0 all-gather.14.cloned.1.call-start
  68.4 0.0 all-gather.22.cloned.1.call-done
  68.4 0.0 copy-start
  68.4 109.4 %all-gather.12.cloned.1.call-done = bf16[4096,1024]{1,0:T(8,128)(2,1)} async-done(((bf16[512,1024]{1,0:T(8,128)(2,1)}), bf16[4096,1024]{1,0:T(8,128)(2,1)}) %all-gather.12.cloned.1.call-update) | async-done | bytes 8388624 | tf_op jit(solution)/shard_map/all_gather | solution.py:24
  177.9 7.2 %fusion.13 = bf16[256,1024]{1,0:T(8,128)(2,1)} fusion(bf16[4096,1024]{1,0:T(8,128)(2,1)} %all-gather.12.cloned.1.call-done, bf16[1,256,4096]{2,1,0:T(8,128)(2,1)} %all-gather.22.cloned.1.call-done), kind=kOutput, calls=%fused_computation.16 | convolution fusion | flops 2147745792 | bytes 11010048 | tf_op jit(solution)/shard_map/dot_general | solution.py:10
  185.0 0.0 all-gather.14.cloned.1.call-update
  185.1 0.0 all-gather.18.cloned.1.call-start
  185.1 117.5 %all-gather.16.cloned.1.call-done = bf16[4096,1024]{1,0:T(8,128)(2,1)} async-done(((bf16[512,1024]{1,0:T(8,128)(2,1)}), bf16[4096,1024]{1,0:T(8,128)(2,1)}) %all-gather.16.cloned.1.call-update) | async-done | bytes 8388624 | tf_op jit(solution)/shard_map/all_gather | solution.py:25
  302.6 0.0 copy-done
  302.6 6.5 %fusion.16 = bf16[256,1024]{1,0:T(8,128)(2,1)} fusion(bf16[4096,1024]{1,0:T(8,128)(2,1)} %all-gather.16.cloned.1.call-done, bf16[1,256,4096]{2,1,0:T(8,128)(2,1)S(1)} %copy-done), kind=kOutput, calls=%fused_computation.17 | convolution fusion | flops 2147745792 | bytes 11010048 | tf_op jit(solution)/shard_map/dot_general | solution.py:10
  309.1 0.0 all-gather.18.cloned.1.call-update
  309.1 16.7 %all-gather.20.cloned.1.call-done = bf16[1,256,4096]{2,1,0:T(8,128)(2,1)} async-done(((bf16[1,256,1024]{2,1,0:T(8,128)(2,1)}), bf16[1,256,4096]{2,1,0:T(8,128)(2,1)}) %all-gather.20.cloned.1.call-update) | async-done | bytes 2097168 | tf_op jit(solution)/shard_map/all_gather | solution.py:35
  325.8 126.0 %all-gather.10.cloned.1.call-done = bf16[4096,1024]{1,0:T(8,128)(2,1)} async-done(((bf16[512,1024]{1,0:T(8,128)(2,1)}), bf16[4096,1024]{1,0:T(8,128)(2,1)}) %all-gather.10.cloned.1.call-update) | async-done | bytes 8388624 | tf_op jit(solution)/shard_map/all_gather | solution.py:23
  451.8 6.3 %fusion.10 = bf16[256,1024]{1,0:T(8,128)(2,1)S(1)} fusion(bf16[4096,1024]{1,0:T(8,128)(2,1)} %all-gather.10.cloned.1.call-done, bf16[1,256,4096]{2,1,0:T(8,128)(2,1)} %all-gather.20.cloned.1.call-done), kind=kOutput, calls=%fused_computation.15 | convolution fusion | flops 2147745792 | bytes 11010048 | tf_op jit(solution)/shard_map/dot_general | solution.py:10
  458.1 16.5 %all-gather.14.cloned.1.call-done = bf16[512,1024]{1,0:T(8,128)(2,1)} async-done(((bf16[256,1024]{1,0:T(8,128)(2,1)}), bf16[512,1024]{1,0:T(8,128)(2,1)}) %all-gather.14.cloned.1.call-update) | async-done | bytes 1048592 | tf_op jit(solution)/shard_map/all_gather | solution.py:42
  474.6 1.8 multiply_reduce_fusion
  476.4 0.6 fusion.6
  476.9 20.3 %all-gather.18.cloned.1.call-done = bf16[512,1024]{1,0:T(8,128)(2,1)} async-done(((bf16[256,1024]{1,0:T(8,128)(2,1)}), bf16[512,1024]{1,0:T(8,128)(2,1)}) %all-gather.18.cloned.1.call-update) | async-done | bytes 1048592 | tf_op jit(solution)/shard_map/all_gather | solution.py:43
  497.3 1.5 copy.11
  498.8 1.5 fusion.9
  500.2 2.0 copy.10
  (3 shorter events, 0.0 us)
Async XLA Ops:
  7.4 60.2 %reduce-scatter.2.cloned.1.call-start = ((), (), s32[]{:S(2)}) async-start(), calls=%async_computation.1 | async-start | bytes 2621440 | tf_op jit(solution)/shard_map/reduce_scatter | solution.py:19
  23.3 45.1 %all-gather.22.cloned.1.call-start = ((), (), s32[]{:S(2)}) async-start(), calls=%async_computation.8 | async-start | bytes 2621440 | tf_op jit(solution)/shard_map/all_gather | solution.py:32
  23.9 154.0 %all-gather.12.cloned.1.call-start = ((), (), s32[]{:S(2)}) async-start(), calls=%async_computation.3 | async-start | bytes 9437184 | tf_op jit(solution)/shard_map/all_gather | solution.py:24
  24.5 278.1 %all-gather.16.cloned.1.call-start = ((), (), s32[]{:S(2)}) async-start(), calls=%async_computation.5 | async-start | bytes 9437184 | tf_op jit(solution)/shard_map/all_gather | solution.py:25
  25.1 300.7 %all-gather.20.cloned.1.call-start = ((), (), s32[]{:S(2)}) async-start(), calls=%async_computation.7 | async-start | bytes 2621440 | tf_op jit(solution)/shard_map/all_gather | solution.py:35
  67.6 384.1 %all-gather.10.cloned.1.call-start = ((), (), s32[]{:S(2)}) async-start(), calls=%async_computation.2 | async-start | bytes 9437184 | tf_op jit(solution)/shard_map/all_gather | solution.py:23
  68.4 406.2 %all-gather.14.cloned.1.call-start = ((), (), s32[]{:S(2)}) async-start(), calls=%async_computation.4 | async-start | bytes 1572864 | tf_op jit(solution)/shard_map/all_gather | solution.py:42
  68.4 234.1 %copy-start = (bf16[1,256,4096]{2,1,0:T(8,128)(2,1)S(1)}, bf16[1,256,4096]{2,1,0:T(8,128)(2,1)}, u32[]{:S(2)}) copy-start(bf16[1,256,4096]{2,1,0:T(8,128)(2,1)} %all-gather.22.cloned.1.call-done) | copy-start | bytes 6291460
  185.1 312.2 %all-gather.18.cloned.1.call-start = ((), (), s32[]{:S(2)}) async-start(), calls=%async_computation.6 | async-start | bytes 1572864 | tf_op jit(solution)/shard_map/all_gather | solution.py:43
Sparse Core Ops, SparseCore 0:
  23.4 44.0 reduce-scatter.1
Sparse Core Ops, SparseCore 1:
  25.3 22.6 all-gather.21
  50.0 127.8 all-gather.11
  179.9 122.6 all-gather.15
  304.2 21.5 all-gather.19
  328.2 123.5 all-gather.9
  453.4 21.1 all-gather.13
  476.1 21.1 all-gather.17
where the time goes:
time: 512 us; the launch traced here: 510 us
  waiting for transfers between devices  451 us (88%)
  matrix products  23.2 us (5%)
  local copies, waits for them, and re-layouts  16.3 us (3%)
  between operations  15 us (3%)
    all_gather x1, waiting for transfers between devices, on_device(): lax.all_gather(w_query, ('section', 'dp'), axis=0, tiled=True)  126 us
    all_gather x1, waiting for transfers between devices, on_device(): lax.all_gather(w_value, ('section', 'dp'), axis=0, tiled=True)  117 us
    all_gather x1, waiting for transfers between devices, on_device(): lax.all_gather(w_key, ('section', 'dp'), axis=0, tiled=True)  109 us
    reduce_scatter x1, waiting for transfers between devices, on_device(): lax.psum_scatter(partial_rows.astype(jnp.bfloat16), 'dp', scatter_dimensi...  42.5 us
    all_gather x1, waiting for transfers between devices, on_device(): lax.all_gather(values_local, 'section', axis=0, tiled=True)  20.3 us
    dot_general x3, matrix products, contract(): return jnp.dot(segment, weight, preferred_element_type=jnp.float32)  20 us
    all_gather x1, waiting for transfers between devices, on_device(): lax.all_gather(decoder_rows, 'tensor', axis=1, tiled=True)  16.7 us
    all_gather x1, waiting for transfers between devices, on_device(): lax.all_gather(keys_local, 'section', axis=0, tiled=True)  16.5 us
  transfers between devices with their start and end apart: 8, of which 7 were waited for; matrix products, arithmetic and copies ran while one was open for 4% of the time, Pallas kernels for 0%

commit v1 on v0

v1 whole, which is shorter than its diff:
```python
import jax
import jax.numpy as jnp
from jax import lax
from jax.sharding import PartitionSpec as P

HD = 256


def contract(segment, weight):
    return jnp.dot(segment, weight, preferred_element_type=jnp.float32)


def make(mesh):
    sections, tensors, planes = (mesh.shape[a] for a in ("section", "tensor", "dp"))

    def to_planes(rows):
        positions = rows.shape[0]
        mine = lax.all_to_all(rows, "tensor", split_axis=0, concat_axis=1, tiled=True)
        depth = mine.shape[1] // (sections * planes)
        mine = mine.reshape(positions // tensors, sections, planes, depth)
        mine = jnp.transpose(mine, (2, 0, 1, 3)).reshape(planes, positions // tensors, sections * depth)
        mine = lax.all_to_all(mine, "dp", split_axis=0, concat_axis=0, tiled=True)
        return lax.all_gather(mine, "tensor", axis=1, tiled=True)

    def project(sources, weights):
        plane = lax.axis_index("dp")

        def partial(index):
            index = jnp.clip(index, 0, planes - 1)
            block = lax.dynamic_index_in_dim(sources, index, 0, keepdims=False)
            return [contract(block, weight) for weight in weights]

        above = below = None
        for step in range(planes - 1):
            away = planes - 1 - step
            up, down = partial(plane + away), partial(plane - away)
            if above is not None:
                up = [a + b for a, b in zip(up, below)]
                down = [a + b for a, b in zip(down, above)]
            up_pairs = [(i, i + 1) for i in range(step + 1)]
            down_pairs = [(planes - 1 - i, planes - 2 - i) for i in range(step + 1)]
            below = [lax.ppermute(a.astype(jnp.bfloat16), "dp", up_pairs).astype(jnp.float32) for a in up]
            above = [lax.ppermute(a.astype(jnp.bfloat16), "dp", down_pairs).astype(jnp.float32) for a in down]
        own = partial(plane)
        if above is not None:
            own = [a + b + c for a, b, c in zip(own, above, below)]
        return [a.astype(jnp.bfloat16) for a in own]

    def on_device(target_ids, embed_table, encoder_out, w_query, w_key, w_value):
        table_rows = embed_table.shape[0]
        offset_ids = target_ids - lax.axis_index("dp") * table_rows
        inside = (offset_ids >= 0) & (offset_ids < table_rows)
        picked = jnp.take(embed_table, jnp.clip(offset_ids, 0, table_rows - 1), axis=0)
        picked = jnp.where(inside[..., None], picked, jnp.zeros((), picked.dtype))
        key_weight, value_weight, query_weight = (
            lax.all_gather(w, "section", axis=0, tiled=True) for w in (w_key, w_value, w_query)
        )
        memory = to_planes(encoder_out[0])
        keys_local, values_local = project(memory, (key_weight, value_weight))
        key_rows = lax.all_gather(keys_local, "section", axis=0, tiled=True)
        value_rows = lax.all_gather(values_local, "section", axis=0, tiled=True)
        decoder_in = lax.psum_scatter(picked, "dp", scatter_dimension=0, tiled=True)
        (queries,) = project(to_planes(decoder_in[0]), (query_weight,))
        positions, columns = queries.shape
        heads_here = columns // HD
        query_heads = queries.reshape(positions, heads_here, HD)
        key_block = key_rows.reshape(-1, heads_here, HD)
        value_block = value_rows.reshape(-1, heads_here, HD)
        scores = (
            jnp.einsum("phd,nhd->hpn", query_heads, key_block, preferred_element_type=jnp.float32)
            * HD ** (-0.5)
        )
        weights = jnp.exp(scores - jnp.max(scores, axis=-1, keepdims=True))
        weight_sum = jnp.sum(weights, axis=-1)
        total = jnp.einsum(
            "hpn,nhd->hpd", weights.astype(jnp.bfloat16), value_block, preferred_element_type=jnp.float32
        )
        result = jnp.transpose(total / weight_sum[..., None], (1, 0, 2))
        return result.reshape(positions, columns).astype(jnp.bfloat16)[None]

    return on_device


def solution(mesh):
    in_specs = (
        P(None, "section"),
        P("dp", "tensor"),
        P("dp", "section", "tensor"),
        P(("section", "dp"), "tensor"),
        P(("section", "dp"), "tensor"),
        P(("section", "dp"), "tensor"),
    )
    out_specs = P("dp", "section", "tensor")
    return jax.shard_map(
        make(mesh), mesh=mesh, in_specs=in_specs, out_specs=out_specs, check_vma=False
    )
```

time: 512 us -> 286 us (0.56)
  waiting for transfers between devices: 451 us -> 101 us
  starting transfers between devices: 0.29 us -> 52.7 us
  blocking collectives: 0 us -> 41 us
  matrix products: 23.2 us -> 40.5 us
  other arithmetic: 3.7 us -> 12.5 us
    all_gather x7, waiting for transfers between devices: 406 us -> 41.2 us  [the longest x3 26.8 us: on_device(): lax.all_gather(w, 'section', axis=0, tiled=True)]
    ppermute x0 -> x18, starting transfers between devices: none -> 41.3 us  [the longest x9 28 us: project(): lax.ppermute(a.astype(jnp.bfloat16), 'dp', up_pairs).astype(jnp.float32)]
    all_to_all x0 -> x2, blocking collectives: none -> 41 us  [the longest x1 30.8 us: to_planes(): mine = lax.all_to_all(mine, 'dp', split_axis=0, concat_axis=0, tiled=True)]
    ppermute x0 -> x18, waiting for transfers between devices: none -> 40.2 us  [the longest x9 26 us: project(): lax.ppermute(a.astype(jnp.bfloat16), 'dp', up_pairs).astype(jnp.float32)]
    reduce_scatter x1, waiting for transfers between devices: 42.5 us -> 10.3 us  [on_device(): decoder_in = lax.psum_scatter(picked, 'dp', scatter_dimension=0, tiled=True)]
    dot_general x3 -> x21, matrix products: 20 us -> 38 us  [contract(): return jnp.dot(segment, weight, preferred_element_type=jnp.float32)]
    all_to_all x0 -> x2, starting transfers between devices: none -> 10.9 us  [the longest x1 6.92 us: to_planes(): mine = lax.all_to_all(mine, 'dp', split_axis=0, concat_axis=0, tiled=True)]
    convert_element_type x1 -> x9, other arithmetic: 1.73 us -> 8.94 us  [the longest x3 4.56 us: project(): return [a.astype(jnp.bfloat16) for a in own]]
  transfers between devices with their start and end apart: 8 -> 28, of which waited for: 7 -> 14; matrix products, arithmetic and copies ran while one was open for 4% -> 19% of each run, Pallas kernels for 0% -> 0%
where the time goes in v1:
time: 286 us; the launch traced here: 282 us
  waiting for transfers between devices  101 us (35%)
  starting transfers between devices  52.7 us (18%)
  blocking collectives  41 us (14%)
  matrix products  40.5 us (14%)
  local copies, waits for them, and re-layouts  19.5 us (7%)
  between operations  15.5 us (5%)
  other arithmetic  12.5 us (4%)
    dot_general x21, matrix products, contract(): return jnp.dot(segment, weight, preferred_element_type=jnp.float32)  38 us
    all_to_all x1, blocking collectives, to_planes(): mine = lax.all_to_all(mine, 'dp', split_axis=0, concat_axis=0, tiled=True)  30.8 us
    ppermute x9, starting transfers between devices, project(): lax.ppermute(a.astype(jnp.bfloat16), 'dp', up_pairs).astype(jnp.float32)  28 us
    all_gather x3, waiting for transfers between devices, on_device(): lax.all_gather(w, 'section', axis=0, tiled=True)  26.8 us
    ppermute x9, waiting for transfers between devices, project(): lax.ppermute(a.astype(jnp.bfloat16), 'dp', up_pairs).astype(jnp.float32)  26 us
    all_gather x2, waiting for transfers between devices, to_planes(): return lax.all_gather(mine, 'tensor', axis=1, tiled=True)  14.3 us
    ppermute x9, waiting for transfers between devices, project(): lax.ppermute(a.astype(jnp.bfloat16), 'dp', down_pairs).astype(jnp.float32)  14.2 us
    ppermute x9, starting transfers between devices, project(): lax.ppermute(a.astype(jnp.bfloat16), 'dp', down_pairs).astype(jnp.float32)  13.3 us
  transfers between devices with their start and end apart: 28, of which 14 were waited for; matrix products, arithmetic and copies ran while one was open for 19% of the time, Pallas kernels for 0%

profile of v1, /device:TPU:12, one launch (start us, length us, event | category | flops | bytes accessed | tf_op | source)
XLA Modules:
  0.0 282.3 jit_solution(17070328950408495908)
XLA Ops:
  8.8 12.8 %gather_fusion = bf16[1024,1024]{1,0:T(8,128)(2,1)S(1)} fusion(bf16[8032,1024]{1,0:T(8,128)(2,1)} %param.7, s32[1024]{0:T(1024)S(1)} %broadcast_clamp_fusion), kind=kCustom, calls=%fused_computation | custom fusion | bytes 4198400 | tf_op jit(solution)/shard_map/jit(_take)/gather | solution.py:53
  21.6 1.6 select_select_fusion
  24.1 10.3 %all_to_all.42 = bf16[4,64,1024]{2,1,0:T(8,128)(2,1)S(1)} all-to-all(bf16[4,64,1024]{2,1,0:T(8,128)(2,1)S(1)} %bitcast.129), channel_id=1, replica_groups=mesh['section'=2,'tensor'=4,'dp'=4] {'tensor'}, dimensions={0} | all-to-all | bytes 1048576 | tf_op jit(solution)/shard_map/all_to_all | solution.py:18
  36.0 30.8 %all_to_all.43 = bf16[4,64,1024]{2,1,0:T(8,128)(2,1)} all-to-all(bf16[4,64,1024]{2,1,0:T(8,128)(2,1)S(1)} %reshape.55), channel_id=1, replica_groups=mesh['section'=2,'tensor'=4,'dp'=4] {'dp'}, dimensions={0} | all-to-all | bytes 1048576 | tf_op jit(solution)/shard_map/all_to_all | solution.py:22
  68.1 10.3 %reduce-scatter.2.cloned.1.call-done = bf16[1,256,1024]{2,1,0:T(8,128)(2,1)} async-done(((bf16[4,256,1024]{2,1,0:T(8,128)(2,1)}), bf16[1,256,1024]{2,1,0:T(8,128)(2,1)}) %reduce-scatter.2.cloned.1.call-update) | async-done | bytes 524304 | tf_op jit(solution)/shard_map/reduce_scatter | solution.py:62
  78.4 4.0 %all-to-all-start = ((bf16[4,64,1024]{2,1,0:T(8,128)(2,1)}), bf16[4,64,1024]{2,1,0:T(8,128)(2,1)S(1)}, u32[]{:S(2)}, u32[]{:S(2)}) async-start(bf16[4,64,1024]{2,1,0:T(8,128)(2,1)} %bitcast.130), calls=%async_computation.1 | async-start | bytes 1048576 | tf_op jit(solution)/shard_map/all_to_all | solution.py:18
  82.4 14.3 %all-gather.12.cloned.1.call-done = bf16[4,256,1024]{2,1,0:T(8,128)(2,1)} async-done(((bf16[4,64,1024]{2,1,0:T(8,128)(2,1)}), bf16[4,256,1024]{2,1,0:T(8,128)(2,1)}) %all-gather.12.cloned.1.call-update) | async-done | bytes 2097168 | tf_op jit(solution)/shard_map/all_gather | solution.py:23
  96.7 3.3 %convolution_convert_fusion.2 = bf16[256,1024]{1,0:T(8,128)(2,1)} fusion(bf16[1024,1024]{1,0:T(8,128)(2,1)} %all-gather.14.cloned.1.call-done, bf16[4,256,1024]{2,1,0:T(8,128)(2,1)} %all-gather.12.cloned.1.call-done, s32[]{:T(128)S(6)} %min.45), kind=kOutput, calls=%fused_computation.11 | convolution fusion | flops 537133056 | bytes 3145732 | tf_op jit(solution)/shard_map/dot_general | solution.py:10
  100.0 1.3 collective-permute-start.9
  101.3 2.6 convolution_convert_fusion.3
  103.9 1.5 collective-permute-start.6
  105.3 26.7 %all-gather.18.cloned.1.call-done = bf16[1024,1024]{1,0:T(8,128)(2,1)} async-done(((bf16[512,1024]{1,0:T(8,128)(2,1)}), bf16[1024,1024]{1,0:T(8,128)(2,1)}) %all-gather.18.cloned.1.call-update) | async-done | bytes 2097168 | tf_op jit(solution)/shard_map/all_gather | solution.py:56
  132.1 3.3 %convolution_convert_fusion.1 = bf16[256,1024]{1,0:T(8,128)(2,1)} fusion(bf16[1024,1024]{1,0:T(8,128)(2,1)} %all-gather.18.cloned.1.call-done, bf16[4,256,1024]{2,1,0:T(8,128)(2,1)} %all-gather.12.cloned.1.call-done, s32[]{:T(128)S(6)} %min.42), kind=kOutput, calls=%fused_computation.10 | convolution fusion | flops 537133056 | bytes 3145732 | tf_op jit(solution)/shard_map/dot_general | solution.py:10
  135.3 1.5 collective-permute-start.12
  138.0 1.2 reshape.52
  139.1 6.9 %all-to-all-start.1 = ((bf16[4,64,1024]{2,1,0:T(8,128)(2,1)}), bf16[4,64,1024]{2,1,0:T(8,128)(2,1)}, u32[]{:S(2)}, u32[]{:S(2)}) async-start(bf16[4,64,1024]{2,1,0:T(8,128)(2,1)} %reshape.52), calls=%async_computation.2 | async-start | bytes 1048576 | tf_op jit(solution)/shard_map/all_to_all | solution.py:22
  146.1 3.4 %convolution_convert_fusion = bf16[256,1024]{1,0:T(8,128)(2,1)} fusion(bf16[1024,1024]{1,0:T(8,128)(2,1)} %all-gather.18.cloned.1.call-done, bf16[4,256,1024]{2,1,0:T(8,128)(2,1)} %all-gather.12.cloned.1.call-done, s32[]{:T(128)S(6)} %min.45), kind=kOutput, calls=%fused_computation.9 | convolution fusion | flops 537133056 | bytes 3145732 | tf_op jit(solution)/shard_map/dot_general | solution.py:10
  149.5 1.4 collective-permute-start.15
  151.6 1.7 fusion.36
  153.3 7.1 %all-to-all-done.1 = bf16[4,64,1024]{2,1,0:T(8,128)(2,1)} async-done(((bf16[4,64,1024]{2,1,0:T(8,128)(2,1)}), bf16[4,64,1024]{2,1,0:T(8,128)(2,1)}, u32[]{:S(2)}, u32[]{:S(2)}) %all-to-all-start.1) | async-done | bytes 524320 | tf_op jit(solution)/shard_map/all_to_all | solution.py:22
  160.7 1.9 fusion.24
  162.7 1.9 fusion.22
  165.3 1.8 add_convert_fusion.4
  167.1 1.3 collective-permute-start.13
  168.4 1.8 add_convert_fusion.2
  170.1 4.7 %collective-permute-start.16 = (bf16[256,1024]{1,0:T(8,128)(2,1)S(1)}, bf16[256,1024]{1,0:T(8,128)(2,1)S(1)}, u32[]{:S(2)}, u32[]{:S(2)}) collective-permute-start(bf16[256,1024]{1,0:T(8,128)(2,1)S(1)} %add_convert_fusion.2), channel_id=1, source_target_pairs={{0,1},{1,2},{4,5},{5,6},{8,9},{9,10},{12,13},{13,14},{16,17},{17,1... | collective-permute-start | bytes 1572872 | tf_op jit(solution)/shard_map/ppermute | solution.py:42
  174.8 1.8 add_convert_fusion.7
  176.7 1.9 collective-permute-start.10
  178.6 3.0 %collective-permute-done.13 = bf16[256,1024]{1,0:T(8,128)(2,1)S(1)} collective-permute-done((bf16[256,1024]{1,0:T(8,128)(2,1)S(1)}, bf16[256,1024]{1,0:T(8,128)(2,1)S(1)}, u32[]{:S(2)}, u32[]{:S(2)}) %collective-permute-start.13) | collective-permute-done | bytes 524320 | tf_op jit(solution)/shard_map/ppermute | solution.py:43
  181.8 1.9 collective-permute-start.14
  183.7 3.5 %collective-permute-done.16 = bf16[256,1024]{1,0:T(8,128)(2,1)S(1)} collective-permute-done((bf16[256,1024]{1,0:T(8,128)(2,1)S(1)}, bf16[256,1024]{1,0:T(8,128)(2,1)S(1)}, u32[]{:S(2)}, u32[]{:S(2)}) %collective-permute-start.16) | collective-permute-done | bytes 524320 | tf_op jit(solution)/shard_map/ppermute | solution.py:42
  187.3 4.4 %collective-permute-start.17 = (bf16[256,1024]{1,0:T(8,128)(2,1)S(1)}, bf16[256,1024]{1,0:T(8,128)(2,1)S(1)}, u32[]{:S(2)}, u32[]{:S(2)}) collective-permute-start(bf16[256,1024]{1,0:T(8,128)(2,1)S(1)} %add_convert_fusion.1), channel_id=1, source_target_pairs={{0,1},{1,2},{2,3},{4,5},{5,6},{6,7},{8,9},{9,10},{10,11},{12,13},{... | collective-permute-start | bytes 1572872 | tf_op jit(solution)/shard_map/ppermute | solution.py:42
  191.7 2.6 add_convert_fusion.9
  194.3 1.3 collective-permute-start.7
  195.6 2.8 collective-permute-done.10
  198.4 1.0 add_convert_fusion.6
  199.4 4.4 %collective-permute-start.11 = (bf16[256,1024]{1,0:T(8,128)(2,1)}, bf16[256,1024]{1,0:T(8,128)(2,1)}, u32[]{:S(2)}, u32[]{:S(2)}) collective-permute-start(bf16[256,1024]{1,0:T(8,128)(2,1)} %add_convert_fusion.6), channel_id=1, source_target_pairs={{0,1},{1,2},{2,3},{4,5},{5,6},{6,7},{8,9},{9,10},{10,11},{12,13},{... | collective-permute-start | bytes 1572872 | tf_op jit(solution)/shard_map/ppermute | solution.py:42
  203.8 5.9 %collective-permute-done.17 = bf16[256,1024]{1,0:T(8,128)(2,1)S(1)} collective-permute-done((bf16[256,1024]{1,0:T(8,128)(2,1)S(1)}, bf16[256,1024]{1,0:T(8,128)(2,1)S(1)}, u32[]{:S(2)}, u32[]{:S(2)}) %collective-permute-start.17) | collective-permute-done | bytes 524320 | tf_op jit(solution)/shard_map/ppermute | solution.py:42
  209.7 1.0 add_convert_fusion
  210.8 1.2 add_convert_fusion.8
  212.0 1.9 collective-permute-start.8
  213.9 1.8 fusion.42
  215.7 3.0 %collective-permute-done.11 = bf16[256,1024]{1,0:T(8,128)(2,1)} collective-permute-done((bf16[256,1024]{1,0:T(8,128)(2,1)}, bf16[256,1024]{1,0:T(8,128)(2,1)}, u32[]{:S(2)}, u32[]{:S(2)}) %collective-permute-start.11) | collective-permute-done | bytes 524320 | tf_op jit(solution)/shard_map/ppermute | solution.py:42
  218.7 5.0 %collective-permute-done.8 = bf16[256,1024]{1,0:T(8,128)(2,1)S(1)} collective-permute-done((bf16[256,1024]{1,0:T(8,128)(2,1)S(1)}, bf16[256,1024]{1,0:T(8,128)(2,1)S(1)}, u32[]{:S(2)}, u32[]{:S(2)}) %collective-permute-start.8) | collective-permute-done | bytes 524320 | tf_op jit(solution)/shard_map/ppermute | solution.py:43
  223.6 2.1 add_convert_fusion.5
  225.8 2.6 convolution_convert_fusion.5
  228.4 0.8 collective-permute-start
  229.3 1.8 convolution_convert_fusion.4
  231.0 1.3 collective-permute-start.3
  233.8 1.3 collective-permute-start.1
  235.1 8.2 %collective-permute-done.3 = bf16[256,1024]{1,0:T(8,128)(2,1)S(1)} collective-permute-done((bf16[256,1024]{1,0:T(8,128)(2,1)S(1)}, bf16[256,1024]{1,0:T(8,128)(2,1)S(1)}, u32[]{:S(2)}, u32[]{:S(2)}) %collective-permute-start.3) | collective-permute-done | bytes 524320 | tf_op jit(solution)/shard_map/ppermute | solution.py:42
  244.1 4.2 %collective-permute-start.4 = (bf16[256,1024]{1,0:T(8,128)(2,1)S(1)}, bf16[256,1024]{1,0:T(8,128)(2,1)S(1)}, u32[]{:S(2)}, u32[]{:S(2)}) collective-permute-start(bf16[256,1024]{1,0:T(8,128)(2,1)S(1)} %add_convert_fusion.12), channel_id=1, source_target_pairs={{0,1},{1,2},{4,5},{5,6},{8,9},{9,10},{12,13},{13,14},{16,17},{17,1... | collective-permute-start | bytes 1572872 | tf_op jit(solution)/shard_map/ppermute | solution.py:42
  249.0 5.2 %collective-permute-done.1 = bf16[256,1024]{1,0:T(8,128)(2,1)S(1)} collective-permute-done((bf16[256,1024]{1,0:T(8,128)(2,1)S(1)}, bf16[256,1024]{1,0:T(8,128)(2,1)S(1)}, u32[]{:S(2)}, u32[]{:S(2)}) %collective-permute-start.1) | collective-permute-done | bytes 524320 | tf_op jit(solution)/shard_map/ppermute | solution.py:43
  254.1 1.0 add_convert_fusion.13
  255.1 1.9 collective-permute-start.2
  257.0 1.0 add_convert_fusion.11
  258.0 4.4 %collective-permute-start.5 = (bf16[256,1024]{1,0:T(8,128)(2,1)}, bf16[256,1024]{1,0:T(8,128)(2,1)}, u32[]{:S(2)}, u32[]{:S(2)}) collective-permute-start(bf16[256,1024]{1,0:T(8,128)(2,1)} %add_convert_fusion.11), channel_id=1, source_target_pairs={{0,1},{1,2},{2,3},{4,5},{5,6},{6,7},{8,9},{9,10},{10,11},{12,13},{... | collective-permute-start | bytes 1572872 | tf_op jit(solution)/shard_map/ppermute | solution.py:42
  262.5 1.5 copy.34
  264.0 1.8 fusion.58
  265.7 1.0 collective-permute-done.2
  266.8 2.6 collective-permute-done.5
  269.4 1.4 add_convert_fusion.10
  270.9 1.8 multiply_reduce_fusion
  273.9 1.0 copy.33
  (69 shorter events, 12.6 us)
Async XLA Ops:
  7.4 71.0 %reduce-scatter.2.cloned.1.call-start = ((), (), s32[]{:S(2)}) async-start(), calls=%async_computation.5 | async-start | bytes 2621440 | tf_op jit(solution)/shard_map/reduce_scatter | solution.py:62
  23.1 1.0 copy-start.8
  23.1 59.3 %all-gather.14.cloned.1.call-start = ((), (), s32[]{:S(2)}) async-start(), calls=%async_computation.9 | async-start | bytes 3145728 | tf_op jit(solution)/shard_map/all_gather | solution.py:56
  23.7 73.0 %all-gather.12.cloned.1.call-start = ((), (), s32[]{:S(2)}) async-start(), calls=%async_computation.8 | async-start | bytes 2621440 | tf_op jit(solution)/shard_map/all_gather | solution.py:23
  66.8 65.3 %all-gather.18.cloned.1.call-start = ((), (), s32[]{:S(2)}) async-start(), calls=%async_computation.11 | async-start | bytes 3145728 | tf_op jit(solution)/shard_map/all_gather | solution.py:56
  67.3 158.4 %all-gather.10.cloned.1.call-start = ((), (), s32[]{:S(2)}) async-start(), calls=%async_computation.7 | async-start | bytes 3145728 | tf_op jit(solution)/shard_map/all_gather | solution.py:56
  78.4 58.4 %all-to-all-start = ((bf16[4,64,1024]{2,1,0:T(8,128)(2,1)}), bf16[4,64,1024]{2,1,0:T(8,128)(2,1)S(1)}, u32[]{:S(2)}, u32[]{:S(2)}) async-start(bf16[4,64,1024]{2,1,0:T(8,128)(2,1)} %bitcast.130), calls=%async_computation.1 | async-start | bytes 1048576 | tf_op jit(solution)/shard_map/all_to_all | solution.py:18
  82.4 18.9 %copy-start.1 = (bf16[1024,1024]{1,0:T(8,128)(2,1)S(1)}, bf16[1024,1024]{1,0:T(8,128)(2,1)}, u32[]{:S(2)}) copy-start(bf16[1024,1024]{1,0:T(8,128)(2,1)} %all-gather.14.cloned.1.call-done) | copy-start | bytes 6291460
  100.0 74.8 %collective-permute-start.9 = (bf16[256,1024]{1,0:T(8,128)(2,1)}, bf16[256,1024]{1,0:T(8,128)(2,1)}, u32[]{:S(2)}, u32[]{:S(2)}) collective-permute-start(bf16[256,1024]{1,0:T(8,128)(2,1)} %convolution_convert_fusion.2), channel_id=1, source_target_pairs={{0,1},{4,5},{8,9},{12,13},{16,17},{20,21},{24,25},{28,29}} | collective-permute-start | bytes 1572872 | tf_op jit(solution)/shard_map/ppermute | solution.py:42
  103.9 87.9 %collective-permute-start.6 = (bf16[256,1024]{1,0:T(8,128)(2,1)}, bf16[256,1024]{1,0:T(8,128)(2,1)}, u32[]{:S(2)}, u32[]{:S(2)}) collective-permute-start(bf16[256,1024]{1,0:T(8,128)(2,1)} %convolution_convert_fusion.3), channel_id=1, source_target_pairs={{3,2},{7,6},{11,10},{15,14},{19,18},{23,22},{27,26},{31,30}} | collective-permute-start | bytes 1572872 | tf_op jit(solution)/shard_map/ppermute | solution.py:43
  135.3 29.9 %collective-permute-start.12 = (bf16[256,1024]{1,0:T(8,128)(2,1)}, bf16[256,1024]{1,0:T(8,128)(2,1)}, u32[]{:S(2)}, u32[]{:S(2)}) collective-permute-start(bf16[256,1024]{1,0:T(8,128)(2,1)} %convolution_convert_fusion.1), channel_id=1, source_target_pairs={{3,2},{7,6},{11,10},{15,14},{19,18},{23,22},{27,26},{31,30}} | collective-permute-start | bytes 1572872 | tf_op jit(solution)/shard_map/ppermute | solution.py:43
  139.1 21.3 %all-to-all-start.1 = ((bf16[4,64,1024]{2,1,0:T(8,128)(2,1)}), bf16[4,64,1024]{2,1,0:T(8,128)(2,1)}, u32[]{:S(2)}, u32[]{:S(2)}) async-start(bf16[4,64,1024]{2,1,0:T(8,128)(2,1)} %reshape.52), calls=%async_computation.2 | async-start | bytes 1048576 | tf_op jit(solution)/shard_map/all_to_all | solution.py:22
  146.1 79.7 %all-gather.8.cloned.1.call-start = ((), (), s32[]{:S(2)}) async-start(), calls=%async_computation.6 | async-start | bytes 2621440 | tf_op jit(solution)/shard_map/all_gather | solution.py:23
  146.1 4.8 %copy-start.4 = (bf16[4,256,1024]{2,1,0:T(8,128)(2,1)S(1)}, bf16[4,256,1024]{2,1,0:T(8,128)(2,1)}, u32[]{:S(2)}) copy-start(bf16[4,256,1024]{2,1,0:T(8,128)(2,1)} %all-gather.12.cloned.1.call-done) | copy-start | bytes 6291460
  149.5 2.1 copy-start.2
  149.5 18.9 %collective-permute-start.15 = (bf16[256,1024]{1,0:T(8,128)(2,1)}, bf16[256,1024]{1,0:T(8,128)(2,1)}, u32[]{:S(2)}, u32[]{:S(2)}) collective-permute-start(bf16[256,1024]{1,0:T(8,128)(2,1)} %convolution_convert_fusion), channel_id=1, source_target_pairs={{0,1},{4,5},{8,9},{12,13},{16,17},{20,21},{24,25},{28,29}} | collective-permute-start | bytes 1572872 | tf_op jit(solution)/shard_map/ppermute | solution.py:42
  160.5 102.0 %all-gather.20.cloned.1.call-start = ((), (), s32[]{:S(2)}) async-start(), calls=%async_computation.12 | async-start | bytes 1572864 | tf_op jit(solution)/shard_map/all_gather | solution.py:61
  160.7 1.9 copy-start.3
  162.6 1.9 copy-start.5
  167.1 14.6 %collective-permute-start.13 = (bf16[256,1024]{1,0:T(8,128)(2,1)S(1)}, bf16[256,1024]{1,0:T(8,128)(2,1)S(1)}, u32[]{:S(2)}, u32[]{:S(2)}) collective-permute-start(bf16[256,1024]{1,0:T(8,128)(2,1)S(1)} %add_convert_fusion.4), channel_id=1, source_target_pairs={{3,2},{2,1},{7,6},{6,5},{11,10},{10,9},{15,14},{14,13},{19,18},{18... | collective-permute-start | bytes 1572872 | tf_op jit(solution)/shard_map/ppermute | solution.py:43
  170.1 11.5 %copy-start.6 = (f32[256,1024]{1,0:T(8,128)S(1)}, f32[256,1024]{1,0:T(8,128)}, u32[]{:S(2)}) copy-start(f32[256,1024]{1,0:T(8,128)} %fusion.36) | copy-start | bytes 3145732
  170.1 17.0 %collective-permute-start.16 = (bf16[256,1024]{1,0:T(8,128)(2,1)S(1)}, bf16[256,1024]{1,0:T(8,128)(2,1)S(1)}, u32[]{:S(2)}, u32[]{:S(2)}) collective-permute-start(bf16[256,1024]{1,0:T(8,128)(2,1)S(1)} %add_convert_fusion.2), channel_id=1, source_target_pairs={{0,1},{1,2},{4,5},{5,6},{8,9},{9,10},{12,13},{13,14},{16,17},{17,1... | collective-permute-start | bytes 1572872 | tf_op jit(solution)/shard_map/ppermute | solution.py:42
  176.7 21.8 %collective-permute-start.10 = (bf16[256,1024]{1,0:T(8,128)(2,1)S(1)}, bf16[256,1024]{1,0:T(8,128)(2,1)S(1)}, u32[]{:S(2)}, u32[]{:S(2)}) collective-permute-start(bf16[256,1024]{1,0:T(8,128)(2,1)S(1)} %add_convert_fusion.7), channel_id=1, source_target_pairs={{0,1},{1,2},{4,5},{5,6},{8,9},{9,10},{12,13},{13,14},{16,17},{17,1... | collective-permute-start | bytes 1572872 | tf_op jit(solution)/shard_map/ppermute | solution.py:42
  181.8 22.0 %collective-permute-start.14 = (bf16[256,1024]{1,0:T(8,128)(2,1)S(1)}, bf16[256,1024]{1,0:T(8,128)(2,1)S(1)}, u32[]{:S(2)}, u32[]{:S(2)}) collective-permute-start(bf16[256,1024]{1,0:T(8,128)(2,1)S(1)} %add_convert_fusion.3), channel_id=1, source_target_pairs={{3,2},{2,1},{1,0},{7,6},{6,5},{5,4},{11,10},{10,9},{9,8},{15,14},{... | collective-permute-start | bytes 1572872 | tf_op jit(solution)/shard_map/ppermute | solution.py:43
  187.3 22.3 %collective-permute-start.17 = (bf16[256,1024]{1,0:T(8,128)(2,1)S(1)}, bf16[256,1024]{1,0:T(8,128)(2,1)S(1)}, u32[]{:S(2)}, u32[]{:S(2)}) collective-permute-start(bf16[256,1024]{1,0:T(8,128)(2,1)S(1)} %add_convert_fusion.1), channel_id=1, source_target_pairs={{0,1},{1,2},{2,3},{4,5},{5,6},{6,7},{8,9},{9,10},{10,11},{12,13},{... | collective-permute-start | bytes 1572872 | tf_op jit(solution)/shard_map/ppermute | solution.py:42
  194.3 16.4 %collective-permute-start.7 = (bf16[256,1024]{1,0:T(8,128)(2,1)}, bf16[256,1024]{1,0:T(8,128)(2,1)}, u32[]{:S(2)}, u32[]{:S(2)}) collective-permute-start(bf16[256,1024]{1,0:T(8,128)(2,1)} %add_convert_fusion.9), channel_id=1, source_target_pairs={{3,2},{2,1},{7,6},{6,5},{11,10},{10,9},{15,14},{14,13},{19,18},{18... | collective-permute-start | bytes 1572872 | tf_op jit(solution)/shard_map/ppermute | solution.py:43
  199.4 19.3 %collective-permute-start.11 = (bf16[256,1024]{1,0:T(8,128)(2,1)}, bf16[256,1024]{1,0:T(8,128)(2,1)}, u32[]{:S(2)}, u32[]{:S(2)}) collective-permute-start(bf16[256,1024]{1,0:T(8,128)(2,1)} %add_convert_fusion.6), channel_id=1, source_target_pairs={{0,1},{1,2},{2,3},{4,5},{5,6},{6,7},{8,9},{9,10},{10,11},{12,13},{... | collective-permute-start | bytes 1572872 | tf_op jit(solution)/shard_map/ppermute | solution.py:42
  210.7 60.1 %all-gather.16.cloned.1.call-start = ((), (), s32[]{:S(2)}) async-start(), calls=%async_computation.10 | async-start | bytes 1572864 | tf_op jit(solution)/shard_map/all_gather | solution.py:60
  212.0 11.7 %collective-permute-start.8 = (bf16[256,1024]{1,0:T(8,128)(2,1)S(1)}, bf16[256,1024]{1,0:T(8,128)(2,1)S(1)}, u32[]{:S(2)}, u32[]{:S(2)}) collective-permute-start(bf16[256,1024]{1,0:T(8,128)(2,1)S(1)} %add_convert_fusion.8), channel_id=1, source_target_pairs={{3,2},{2,1},{1,0},{7,6},{6,5},{5,4},{11,10},{10,9},{9,8},{15,14},{... | collective-permute-start | bytes 1572872 | tf_op jit(solution)/shard_map/ppermute | solution.py:43
  225.8 3.5 %copy-start = (bf16[1024,1024]{1,0:T(8,128)(2,1)S(1)}, bf16[1024,1024]{1,0:T(8,128)(2,1)}, u32[]{:S(2)}) copy-start(bf16[1024,1024]{1,0:T(8,128)(2,1)} %all-gather.10.cloned.1.call-done) | copy-start | bytes 6291460
  228.4 3.9 %copy-start.7 = (bf16[4,256,1024]{2,1,0:T(8,128)(2,1)S(1)}, bf16[4,256,1024]{2,1,0:T(8,128)(2,1)}, u32[]{:S(2)}) copy-start(bf16[4,256,1024]{2,1,0:T(8,128)(2,1)} %all-gather.8.cloned.1.call-done) | copy-start | bytes 6291460
  228.4 4.6 %collective-permute-start = (bf16[256,1024]{1,0:T(8,128)(2,1)S(1)}, bf16[256,1024]{1,0:T(8,128)(2,1)S(1)}, u32[]{:S(2)}, u32[]{:S(2)}) collective-permute-start(bf16[256,1024]{1,0:T(8,128)(2,1)S(1)} %convolution_convert_fusion.5), channel_id=1, source_target_pairs={{3,2},{7,6},{11,10},{15,14},{19,18},{23,22},{27,26},{31,30}} | collective-permute-start | bytes 1572872 | tf_op jit(solution)/shard_map/ppermute | solution.py:43
  231.0 12.3 %collective-permute-start.3 = (bf16[256,1024]{1,0:T(8,128)(2,1)S(1)}, bf16[256,1024]{1,0:T(8,128)(2,1)S(1)}, u32[]{:S(2)}, u32[]{:S(2)}) collective-permute-start(bf16[256,1024]{1,0:T(8,128)(2,1)S(1)} %convolution_convert_fusion.4), channel_id=1, source_target_pairs={{0,1},{4,5},{8,9},{12,13},{16,17},{20,21},{24,25},{28,29}} | collective-permute-start | bytes 1572872 | tf_op jit(solution)/shard_map/ppermute | solution.py:42
  233.8 20.3 %collective-permute-start.1 = (bf16[256,1024]{1,0:T(8,128)(2,1)S(1)}, bf16[256,1024]{1,0:T(8,128)(2,1)S(1)}, u32[]{:S(2)}, u32[]{:S(2)}) collective-permute-start(bf16[256,1024]{1,0:T(8,128)(2,1)S(1)} %add_convert_fusion.14), channel_id=1, source_target_pairs={{3,2},{2,1},{7,6},{6,5},{11,10},{10,9},{15,14},{14,13},{19,18},{18... | collective-permute-start | bytes 1572872 | tf_op jit(solution)/shard_map/ppermute | solution.py:43
  244.1 13.0 %collective-permute-start.4 = (bf16[256,1024]{1,0:T(8,128)(2,1)S(1)}, bf16[256,1024]{1,0:T(8,128)(2,1)S(1)}, u32[]{:S(2)}, u32[]{:S(2)}) collective-permute-start(bf16[256,1024]{1,0:T(8,128)(2,1)S(1)} %add_convert_fusion.12), channel_id=1, source_target_pairs={{0,1},{1,2},{4,5},{5,6},{8,9},{9,10},{12,13},{13,14},{16,17},{17,1... | collective-permute-start | bytes 1572872 | tf_op jit(solution)/shard_map/ppermute | solution.py:42
  255.1 11.7 %collective-permute-start.2 = (bf16[256,1024]{1,0:T(8,128)(2,1)}, bf16[256,1024]{1,0:T(8,128)(2,1)}, u32[]{:S(2)}, u32[]{:S(2)}) collective-permute-start(bf16[256,1024]{1,0:T(8,128)(2,1)} %add_convert_fusion.13), channel_id=1, source_target_pairs={{3,2},{2,1},{1,0},{7,6},{6,5},{5,4},{11,10},{10,9},{9,8},{15,14},{... | collective-permute-start | bytes 1572872 | tf_op jit(solution)/shard_map/ppermute | solution.py:43
  258.0 11.4 %collective-permute-start.5 = (bf16[256,1024]{1,0:T(8,128)(2,1)}, bf16[256,1024]{1,0:T(8,128)(2,1)}, u32[]{:S(2)}, u32[]{:S(2)}) collective-permute-start(bf16[256,1024]{1,0:T(8,128)(2,1)} %add_convert_fusion.11), channel_id=1, source_target_pairs={{0,1},{1,2},{2,3},{4,5},{5,6},{6,7},{8,9},{9,10},{10,11},{12,13},{... | collective-permute-start | bytes 1572872 | tf_op jit(solution)/shard_map/ppermute | solution.py:42
Sparse Core Ops, SparseCore 0:
  23.3 55.0 reduce-scatter.1
Sparse Core Ops, SparseCore 1:
  25.1 34.0 all-gather.13
  66.8 29.8 all-gather.11
  98.2 33.8 all-gather.17
  133.6 32.9 all-gather.9
  168.3 21.5 all-gather.7
  210.8 21.2 all-gather.19
  233.5 21.1 all-gather.15

commit v2 on v1

v2 whole, which is shorter than its diff:
```python
import functools

import jax
import jax.numpy as jnp
from jax import lax
from jax.experimental import pallas as pl
from jax.experimental.pallas import tpu as pltpu
from jax.sharding import PartitionSpec as P

HD = 256
KEY, VALUE, QUERY = 0, 1, 2
ENCODER, DECODER = 0, 1


def project_kernel(
    sections, tensors, planes,
    enc, picks, w_key, w_value, w_query,
    q_out, k_out, v_out,
    wbuf, x_enc, x_dec, rs_up, rs_dn, rs_out, sums, up, dn,
    w_local, w_send, w_recv, z_send, z_recv, e_send, e_recv,
    r_send, r_up, r_dn, c_send, c_up, c_dn, o_send, o_recv,
):
    s, t, d = lax.axis_index("section"), lax.axis_index("tensor"), lax.axis_index("dp")
    depth, columns = w_key.shape
    blocks = enc.shape[1] // depth
    groups = planes // blocks
    rank, group = t // groups, lax.rem(t, groups)
    owner = group == d // blocks
    tile = min(columns, 256)
    sent = []

    def remote(src, dst, send_sem, recv_sem, **device):
        return pltpu.make_async_remote_copy(
            src_ref=src, dst_ref=dst, send_sem=send_sem, recv_sem=recv_sem,
            device_id=device, device_id_type=pl.DeviceIdType.MESH,
        )

    def send(when, src, dst, send_sem, recv_sem, **device):
        copy = remote(src, dst, send_sem, recv_sem, **device)
        sent.append((when, copy))

        @pl.when(when)
        def _():
            copy.start()

    def received(dst, recv_sem):
        remote(dst, dst, c_send.at[0, 0], recv_sem, dp=lax.rem(d + 1, planes)).wait_recv()

    always = d >= 0
    barrier = pltpu.get_barrier_semaphore()
    for axis, index, size in (("section", s, sections), ("tensor", t, tensors), ("dp", d, planes)):
        for shift in range(1, size):
            pl.semaphore_signal(
                barrier, inc=1, device_id={axis: lax.rem(index + shift, size)},
                device_id_type=pl.DeviceIdType.MESH,
            )
    pl.semaphore_wait(barrier, sections + tensors + planes - 3)

    def start_weight(j, weight):
        for shift in range(1, sections):
            send(always, weight, wbuf.at[j, s], w_send.at[j, shift], w_recv.at[j, s],
                 section=lax.rem(s + shift, sections))

    def have_weight(j):
        for shift in range(1, sections):
            other = lax.rem(s + shift, sections)
            received(wbuf.at[j, other], w_recv.at[j, other])

    def part(ref, i):
        return ref.at[:, pl.ds(i * depth, depth)]

    for i in range(blocks):
        plane = group * blocks + i
        send(plane != d, part(enc, i), x_enc.at[d, rank], z_send.at[i], z_recv.at[d], dp=plane)
    start_weight(KEY, w_key)
    for i in range(blocks):
        plane = group * blocks + i
        src = picks.at[:, :, pl.ds(i * depth, depth)]
        rising, falling = (d == 0) & (plane > d), (d == planes - 1) & (plane < d)
        send(rising, src, rs_up.at[i], r_send.at[i], r_up.at[i], dp=lax.rem(d + 1, planes))
        send(falling, src, rs_dn.at[i], r_send.at[i], r_dn.at[i], dp=lax.rem(d + planes - 1, planes))
    local = [
        pltpu.make_async_copy(w, wbuf.at[j, s], w_local.at[j])
        for j, w in enumerate((w_key, w_value, w_query))
    ]
    for copy in local:
        copy.start()
    for i in range(blocks):

        @pl.when(group * blocks + i == d)
        def _():
            x_enc[d, rank] = enc[:, pl.ds(i * depth, depth)]

    def clear(ref):
        @pl.loop(0, 3 * planes)
        def _(n):
            ref[n // planes, lax.rem(n, planes)] = jnp.zeros(ref.shape[2:], ref.dtype)

    pl.when(d == 0)(lambda: clear(up))
    pl.when(d == planes - 1)(lambda: clear(dn))

    def spread(kind, buffer):
        for b in sorted(range(planes), key=lambda b: (min(b, planes - 1 - b), -b)):
            if kind == ENCODER:

                @pl.when(owner & (d != b))
                def _():
                    received(buffer.at[b, rank], z_recv.at[b])

            for shift in range(1, tensors):
                send(owner, buffer.at[b, rank], buffer.at[b, rank], e_send.at[kind, b, shift],
                     e_recv.at[kind, b, rank], tensor=lax.rem(t + shift, tensors))

    def have_spread(kind, buffer, b):
        for k in range(sections):

            @pl.when(k * groups + d // blocks != t)
            def _():
                received(buffer.at[b, k], e_recv.at[kind, b, k])

    def forward_rows(stage):
        for i in range(blocks):
            plane = group * blocks + i
            rising, falling = (d == stage) & (plane > d), (d == planes - 1 - stage) & (plane < d)
            for moving, held, sem, to in ((rising, rs_up, r_up, 1), (falling, rs_dn, r_dn, planes - 1)):

                @pl.when(moving)
                def _():
                    received(held.at[i], sem.at[i])

                    @pl.loop(0, planes)
                    def _(b):
                        rs_out[i, b] = picks[b, :, pl.ds(i * depth, depth)] + held[i, b]

                send(moving, rs_out.at[i], held.at[i], r_send.at[i], sem.at[i], dp=lax.rem(d + to, planes))

    def finish_rows():
        for i in range(blocks):
            mine = group * blocks + i == d

            @pl.when(mine)
            def _():
                @pl.loop(0, planes)
                def _(b):
                    x_dec[b, rank] = picks[b, :, pl.ds(i * depth, depth)]

            for has, held, sem in ((d > 0, rs_up, r_up), (d < planes - 1, rs_dn, r_dn)):

                @pl.when(mine & has)
                def _():
                    received(held.at[i], sem.at[i])

                    @pl.loop(0, planes)
                    def _(b):
                        x_dec[b, rank] = x_dec[b, rank] + held[i, b]

    def product(j, x, b, cols):
        total = None
        for k in range(sections):
            term = jnp.dot(x[b, k], wbuf[j, k, :, cols], preferred_element_type=jnp.float32)
            total = term if total is None else total + term
        return total

    def chain(j, x):
        for step in range(planes - 1):
            for b, to, held, sem, has in (
                (planes - 1 - step, 1, up, c_up, d > 0),
                (step, planes - 1, dn, c_dn, d < planes - 1),
            ):
                moving = b > d if to == 1 else b < d

                @pl.when(moving)
                def _():
                    @pl.when(has)
                    def _():
                        received(held.at[j, b], sem.at[j, b])

                    @pl.loop(0, columns // tile)
                    def _(n):
                        cols = pl.ds(pl.multiple_of(n * tile, tile), tile)
                        total = product(j, x, b, cols) + held[j, b, :, cols].astype(jnp.float32)
                        sums[j, b, :, cols] = total.astype(jnp.bfloat16)

                send(moving, sums.at[j, b], held.at[j, b], c_send.at[j, b], sem.at[j, b],
                     dp=lax.rem(d + to, planes))

    def finish(j, x, out):
        @pl.when(d > 0)
        def _():
            received(up.at[j, d], c_up.at[j, d])

        @pl.when(d < planes - 1)
        def _():
            received(dn.at[j, d], c_dn.at[j, d])

        @pl.loop(0, columns // tile)
        def _(n):
            cols = pl.ds(pl.multiple_of(n * tile, tile), tile)
            arrived = up[j, d, :, cols].astype(jnp.float32) + dn[j, d, :, cols].astype(jnp.float32)
            out[:, cols] = (product(j, x, d, cols) + arrived).astype(jnp.bfloat16)

    def share(j, out):
        for shift in range(1, sections):
            send(always, out.at[s], out.at[s], o_send.at[j, shift], o_recv.at[j, s],
                 section=lax.rem(s + shift, sections))

    spread(ENCODER, x_enc)
    forward_rows(1)
    for copy in local:
        copy.wait()
    for b in range(planes):
        have_spread(ENCODER, x_enc, b)
    have_weight(KEY)
    start_weight(VALUE, w_value)
    chain(KEY, x_enc)
    for stage in range(2, planes - 1):
        forward_rows(stage)
    have_weight(VALUE)
    start_weight(QUERY, w_query)
    chain(VALUE, x_enc)
    finish_rows()
    spread(DECODER, x_dec)
    finish(KEY, x_enc, k_out.at[s])
    have_weight(QUERY)
    share(KEY, k_out)
    for b in range(planes):
        have_spread(DECODER, x_dec, b)
    chain(QUERY, x_dec)
    finish(VALUE, x_enc, v_out.at[s])
    share(VALUE, v_out)
    finish(QUERY, x_dec, q_out)
    for j, out in ((KEY, k_out), (VALUE, v_out)):
        for shift in range(1, sections):
            other = lax.rem(s + shift, sections)
            received(out.at[other], o_recv.at[j, other])
    for when, copy in sent:
        pl.when(when)(copy.wait_send)


def projections(mesh, enc, picks, w_key, w_value, w_query):
    sections, tensors, planes = (mesh.shape[a] for a in ("section", "tensor", "dp"))
    positions = enc.shape[0]
    depth, columns = w_key.shape
    blocks = enc.shape[1] // depth
    bf16 = jnp.bfloat16
    dma = pltpu.SemaphoreType.DMA
    rows = (planes, sections, positions, depth)
    moving = (blocks, planes, positions, depth)
    chains = (3, planes, positions, columns)
    vmem = pl.BlockSpec(memory_space=pltpu.VMEM)
    hbm = pl.BlockSpec(memory_space=pl.ANY)
    return pl.pallas_call(
        functools.partial(project_kernel, sections, tensors, planes),
        out_shape=(
            jax.ShapeDtypeStruct((positions, columns), bf16),
            jax.ShapeDtypeStruct((sections, positions, columns), bf16),
            jax.ShapeDtypeStruct((sections, positions, columns), bf16),
        ),
        in_specs=[vmem, vmem, hbm, hbm, hbm],
        out_specs=(vmem, vmem, vmem),
        scratch_shapes=[
            pltpu.VMEM((3, sections, depth, columns), bf16),
            pltpu.VMEM(rows, bf16),
            pltpu.VMEM(rows, bf16),
            pltpu.VMEM(moving, bf16),
            pltpu.VMEM(moving, bf16),
            pltpu.VMEM(moving, bf16),
            pltpu.VMEM(chains, bf16),
            pltpu.VMEM(chains, bf16),
            pltpu.VMEM(chains, bf16),
            dma((3,)),
            dma((3, sections)),
            dma((3, sections)),
            dma((blocks,)),
            dma((planes,)),
            dma((2, planes, tensors)),
            dma((2, planes, sections)),
            dma((blocks,)),
            dma((blocks,)),
            dma((blocks,)),
            dma((3, planes)),
            dma((3, planes)),
            dma((3, planes)),
            dma((2, sections)),
            dma((2, sections)),
        ],
        compiler_params=pltpu.CompilerParams(
            collective_id=0, has_side_effects=True, vmem_limit_bytes=56 * 2**20
        ),
        cost_estimate=pl.CostEstimate(
            flops=6 * planes * positions * sections * depth * columns,
            bytes_accessed=2 * (picks.size + 3 * w_key.size),
            transcendentals=0,
        ),
    )(enc, picks, w_key, w_value, w_query)


def make(mesh):
    def on_device(target_ids, embed_table, encoder_out, w_query, w_key, w_value):
        table_rows = embed_table.shape[0]
        offset_ids = target_ids - lax.axis_index("dp") * table_rows
        inside = (offset_ids >= 0) & (offset_ids < table_rows)
        picked = jnp.take(embed_table, jnp.clip(offset_ids, 0, table_rows - 1), axis=0)
        picked = jnp.where(inside[..., None], picked, jnp.zeros((), picked.dtype))
        queries, key_rows, value_rows = projections(mesh, encoder_out[0], picked, w_key, w_value, w_query)
        positions, columns = queries.shape
        heads_here = columns // HD
        query_heads = queries.reshape(positions, heads_here, HD)
        key_block = key_rows.reshape(-1, heads_here, HD)
        value_block = value_rows.reshape(-1, heads_here, HD)
        scores = (
            jnp.einsum("phd,nhd->hpn", query_heads, key_block, preferred_element_type=jnp.float32)
            * HD ** (-0.5)
        )
        weights = jnp.exp(scores - jnp.max(scores, axis=-1, keepdims=True))
        weight_sum = jnp.sum(weights, axis=-1)
        total = jnp.einsum(
            "hpn,nhd->hpd", weights.astype(jnp.bfloat16), value_block, preferred_element_type=jnp.float32
        )
        result = jnp.transpose(total / weight_sum[..., None], (1, 0, 2))
        return result.reshape(positions, columns).astype(jnp.bfloat16)[None]

    return on_device


def solution(mesh):
    in_specs = (
        P(None, "section"),
        P("dp", "tensor"),
        P("dp", "section", "tensor"),
        P(("section", "dp"), "tensor"),
        P(("section", "dp"), "tensor"),
        P(("section", "dp"), "tensor"),
    )
    out_specs = P("dp", "section", "tensor")
    return jax.shard_map(
        make(mesh), mesh=mesh, in_specs=in_specs, out_specs=out_specs, check_vma=False
    )
```

time: 286 us -> 210 us (0.73)
  the two profiles are of different devices: /device:TPU:12 before, /device:TPU:9 now
where the time goes in v2:
time: 210 us
  Pallas kernels  185 us (88%)
  local copies, waits for them, and re-layouts  17.9 us (9%)
  matrix products  3.61 us (2%)
  other arithmetic  3.52 us (2%)
    pallas_call x1, Pallas kernels, projections(): pl.pallas_call(functools.partial(project_kernel, sections, tensors, plane...  185 us
    gather x1, local copies, waits for them, and re-layouts, on_device(): jnp.take(embed_table, jnp.clip(offset_ids, 0, table_rows - 1), axis=0)  12.8 us

profile of v2, /device:TPU:9, one launch (start us, length us, event | category | flops | bytes accessed | tf_op | source)
XLA Modules:
  0.0 209.6 jit_solution(14027299559730008182)
XLA Ops:
  0.0 0.7 compare_and_fusion.1
  0.7 0.7 fusion.12
  1.4 12.8 %gather_fusion = bf16[1024,1024]{1,0:T(8,128)(2,1)S(1)} fusion(bf16[8032,1024]{1,0:T(8,128)(2,1)} %param.7, s32[1024]{0:T(1024)S(1)} %broadcast_clamp_fusion), kind=kCustom, calls=%fused_computation | custom fusion | bytes 4198400 | tf_op jit(solution)/shard_map/jit(_take)/gather | solution.py:303
  14.2 1.6 select_select_fusion.picks
  15.8 184.6 %shard_map.64 = (bf16[256,1024]{1,0:T(8,128)(2,1)}, bf16[2,256,1024]{2,1,0:T(8,128)(2,1)}, bf16[2,256,1024]{2,1,0:T(8,128)(2,1)}) custom-call(bf16[256,1024]{1,0:T(8,128)(2,1)} %bitcast.24, bf16[4,256,1024]{2,1,0:T(8,128)(2,1)} %select_select_fusion.picks, bf16[512,1024]{1,0:T(8,128)(2,1)} %w_key.1, bf16[512,1024]{1,0:T(8,128)(2,1)} %w_value.1, ...), custom_call_target="tpu_custom_call" | custom-call | flops 6442450944 | bytes 5242880 | tf_op jit(solution)/shard_map/pallas_call | solution.py:252
  200.4 1.9 reshape.30
  202.2 1.6 multiply_reduce_fusion
  203.8 0.0 copy-start
  203.8 0.5 fusion
  204.4 0.7 copy-done
  205.0 1.6 reshape.31
  206.6 2.0 fusion.3
  208.6 1.0 copy.10
  (2 shorter events, 0.0 us)
Async XLA Ops:
  203.8 1.2 copy-start

commit v3 on v2

v3 whole, which is shorter than its diff:
```python
import functools

import jax
import jax.numpy as jnp
from jax import lax
from jax.experimental import pallas as pl
from jax.experimental.pallas import tpu as pltpu
from jax.sharding import PartitionSpec as P

HD = 256
KEY, VALUE, QUERY = 0, 1, 2
ENCODER, DECODER = 0, 1


def project_kernel(
    sections, tensors, planes,
    enc, picks, w_key, w_value, w_query,
    out,
    k_all, v_all, wbuf, x_enc, x_dec, rs_up, rs_dn, rs_out, sums, up, dn,
    w_local, w_send, w_recv, z_send, z_recv, e_send, e_recv,
    r_send, r_up, r_dn, c_send, c_up, c_dn, o_send, o_recv,
):
    s, t, d = lax.axis_index("section"), lax.axis_index("tensor"), lax.axis_index("dp")
    depth, columns = w_key.shape
    blocks = enc.shape[1] // depth
    groups = planes // blocks
    rank, group = t // groups, lax.rem(t, groups)
    owner = group == d // blocks
    chunks = columns // HD
    edge = (d == 0) | (d == planes - 1)
    sent = []

    def remote(src, dst, send_sem, recv_sem, **device):
        return pltpu.make_async_remote_copy(
            src_ref=src, dst_ref=dst, send_sem=send_sem, recv_sem=recv_sem,
            device_id=device, device_id_type=pl.DeviceIdType.MESH,
        )

    def send(when, src, dst, send_sem, recv_sem, **device):
        copy = remote(src, dst, send_sem, recv_sem, **device)
        sent.append((when, copy))

        @pl.when(when)
        def _():
            copy.start()

    def received(dst, recv_sem):
        remote(dst, dst, c_send.at[0, 0, 0], recv_sem, dp=lax.rem(d + 1, planes)).wait_recv()

    always = d >= 0
    barrier = pltpu.get_barrier_semaphore()
    for axis, index, size in (("section", s, sections), ("tensor", t, tensors), ("dp", d, planes)):
        for shift in range(1, size):
            pl.semaphore_signal(
                barrier, inc=1, device_id={axis: lax.rem(index + shift, size)},
                device_id_type=pl.DeviceIdType.MESH,
            )
    pl.semaphore_wait(barrier, sections + tensors + planes - 3)

    def start_weight(j, weight):
        for shift in range(1, sections):
            send(always, weight, wbuf.at[j, s], w_send.at[j, shift], w_recv.at[j, s],
                 section=lax.rem(s + shift, sections))

    def have_weight(j):
        for shift in range(1, sections):
            other = lax.rem(s + shift, sections)
            received(wbuf.at[j, other], w_recv.at[j, other])

    def part(ref, i):
        return ref.at[:, pl.ds(i * depth, depth)]

    for i in range(blocks):
        plane = group * blocks + i
        send(plane != d, part(enc, i), x_enc.at[d, rank], z_send.at[i], z_recv.at[d], dp=plane)
    start_weight(KEY, w_key)
    for order, held, sem, end, to in (
        (reversed(range(blocks)), rs_up, r_up, 0, 1),
        (range(blocks), rs_dn, r_dn, planes - 1, planes - 1),
    ):
        for i in order:
            plane = group * blocks + i
            moving = (d == end) & ((plane > d) if to == 1 else (plane < d))
            for b in range(planes):
                src = picks.at[b, :, pl.ds(i * depth, depth)]
                send(moving, src, held.at[i, b], r_send.at[i, b], sem.at[i, b], dp=lax.rem(d + to, planes))
    local = [
        pltpu.make_async_copy(w, wbuf.at[j, s], w_local.at[j])
        for j, w in enumerate((w_key, w_value, w_query))
    ]
    for copy in local:
        copy.start()
    for i in range(blocks):

        @pl.when(group * blocks + i == d)
        def _():
            x_enc[d, rank] = enc[:, pl.ds(i * depth, depth)]

    def clear(ref):
        @pl.loop(0, 3 * planes)
        def _(n):
            ref[n // planes, lax.rem(n, planes)] = jnp.zeros(ref.shape[2:], ref.dtype)

    pl.when(d == 0)(lambda: clear(up))
    pl.when(d == planes - 1)(lambda: clear(dn))

    def spread(kind, buffer):
        for b in sorted(range(planes), key=lambda b: (min(b, planes - 1 - b), -b)):
            if kind == ENCODER:

                @pl.when(owner & (d != b))
                def _():
                    received(buffer.at[b, rank], z_recv.at[b])

            else:
                finish_rows(b)
            for shift in range(1, tensors):
                send(owner, buffer.at[b, rank], buffer.at[b, rank], e_send.at[kind, b, shift],
                     e_recv.at[kind, b, rank], tensor=lax.rem(t + shift, tensors))

    def have_spread(kind, buffer, b):
        for k in range(sections):

            @pl.when(k * groups + d // blocks != t)
            def _():
                received(buffer.at[b, k], e_recv.at[kind, b, k])

    def forward_rows():
        for order, held, sem, has, to in (
            (reversed(range(blocks)), rs_up, r_up, d > 0, 1),
            (range(blocks), rs_dn, r_dn, d < planes - 1, planes - 1),
        ):
            for i in order:
                plane = group * blocks + i
                moving = has & ((plane > d) if to == 1 else (plane < d))
                for b in range(planes):

                    @pl.when(moving)
                    def _():
                        received(held.at[i, b], sem.at[i, b])
                        rs_out[i, b] = picks[b, :, pl.ds(i * depth, depth)] + held[i, b]

                    send(moving, rs_out.at[i, b], held.at[i, b], r_send.at[i, b], sem.at[i, b],
                         dp=lax.rem(d + to, planes))

    def finish_rows(b):
        for i in range(blocks):
            mine = group * blocks + i == d

            @pl.when(mine)
            def _():
                x_dec[b, rank] = picks[b, :, pl.ds(i * depth, depth)]

            for has, held, sem in ((d > 0, rs_up, r_up), (d < planes - 1, rs_dn, r_dn)):

                @pl.when(mine & has)
                def _():
                    received(held.at[i, b], sem.at[i, b])
                    x_dec[b, rank] = x_dec[b, rank] + held[i, b]

    def product(j, x, b, n):
        cols = pl.ds(pl.multiple_of(n * HD, HD), HD)
        total = None
        for k in range(sections):
            term = jnp.dot(x[b, k], wbuf[j, k, :, cols], preferred_element_type=jnp.float32)
            total = term if total is None else total + term
        return total

    def chain(j, x, gate):
        for step in range(planes - 1):
            for b, to, held, sem, has in (
                (planes - 1 - step, 1, up, c_up, d > 0),
                (step, planes - 1, dn, c_dn, d < planes - 1),
            ):

                @pl.when(gate & (b > d if to == 1 else b < d))
                def _():
                    @pl.loop(0, chunks)
                    def _(n):
                        @pl.when(has)
                        def _():
                            received(held.at[j, b, n], sem.at[j, b, n])

                        total = product(j, x, b, n) + held[j, b, n].astype(jnp.float32)
                        sums[j, b, n] = total.astype(jnp.bfloat16)
                        remote(sums.at[j, b, n], held.at[j, b, n], c_send.at[j, b, n], sem.at[j, b, n],
                               dp=lax.rem(d + to, planes)).start()

    def whole(j, x, n):
        total = product(j, x, d, n)

        @pl.when(d > 0)
        def _():
            received(up.at[j, d, n], c_up.at[j, d, n])

        @pl.when(d < planes - 1)
        def _():
            received(dn.at[j, d, n], c_dn.at[j, d, n])

        rest = up[j, d, n].astype(jnp.float32) + dn[j, d, n].astype(jnp.float32)
        return (total + rest).astype(jnp.bfloat16)

    def finish(j, x, result):
        @pl.loop(0, chunks)
        def _(n):
            result[:, pl.ds(pl.multiple_of(n * HD, HD), HD)] = whole(j, x, n)

    def attend():
        @pl.loop(0, chunks)
        def _(head):
            cols = pl.ds(pl.multiple_of(head * HD, HD), HD)
            queries = whole(QUERY, x_dec, head)
            scores = [
                lax.dot_general(queries, k_all[k, :, cols], (((1,), (1,)), ((), ())),
                                preferred_element_type=jnp.float32) * HD ** (-0.5)
                for k in range(sections)
            ]
            peak = functools.reduce(jnp.maximum, [jnp.max(a, axis=-1, keepdims=True) for a in scores])
            weights = [jnp.exp(a - peak) for a in scores]
            weight_sum = sum(jnp.sum(a, axis=-1, keepdims=True) for a in weights)
            total = sum(
                jnp.dot(a.astype(jnp.bfloat16), v_all[k, :, cols], preferred_element_type=jnp.float32)
                for k, a in enumerate(weights)
            )
            out[:, cols] = (total / weight_sum).astype(jnp.bfloat16)

    def share(j, result):
        for shift in range(1, sections):
            send(always, result.at[s], result.at[s], o_send.at[j, shift], o_recv.at[j, s],
                 section=lax.rem(s + shift, sections))

    spread(ENCODER, x_enc)
    start_weight(VALUE, w_value)
    forward_rows()

    def keys(gate):
        @pl.when(gate)
        def _():
            for b in range(planes):
                have_spread(ENCODER, x_enc, b)
            have_weight(KEY)
            local[KEY].wait()

        chain(KEY, x_enc, gate)

    keys(edge)
    spread(DECODER, x_dec)
    keys(jnp.logical_not(edge))
    local[VALUE].wait()
    local[QUERY].wait()
    have_weight(VALUE)
    start_weight(QUERY, w_query)
    chain(VALUE, x_enc, always)
    finish(KEY, x_enc, k_all.at[s])
    share(KEY, k_all)
    for b in range(planes):
        have_spread(DECODER, x_dec, b)
    have_weight(QUERY)
    chain(QUERY, x_dec, always)
    finish(VALUE, x_enc, v_all.at[s])
    share(VALUE, v_all)
    for j, result in ((KEY, k_all), (VALUE, v_all)):
        for shift in range(1, sections):
            other = lax.rem(s + shift, sections)
            received(result.at[other], o_recv.at[j, other])
    attend()
    for when, copy in sent:
        pl.when(when)(copy.wait_send)
    for j in range(3):
        for b in range(planes):

            @pl.when(b != d)
            def _():
                @pl.loop(0, chunks)
                def _(n):
                    remote(sums.at[j, b, n], sums.at[j, b, n], c_send.at[j, b, n], c_up.at[j, b, n],
                           dp=lax.rem(d + 1, planes)).wait_send()


def projections(mesh, enc, picks, w_key, w_value, w_query):
    sections, tensors, planes = (mesh.shape[a] for a in ("section", "tensor", "dp"))
    positions = enc.shape[0]
    depth, columns = w_key.shape
    blocks = enc.shape[1] // depth
    bf16 = jnp.bfloat16
    dma = pltpu.SemaphoreType.DMA
    rows = (planes, sections, positions, depth)
    moving = (blocks, planes, positions, depth)
    chains = (3, planes, columns // HD, positions, HD)
    vmem = pl.BlockSpec(memory_space=pltpu.VMEM)
    hbm = pl.BlockSpec(memory_space=pl.ANY)
    return pl.pallas_call(
        functools.partial(project_kernel, sections, tensors, planes),
        out_shape=jax.ShapeDtypeStruct((positions, columns), bf16),
        in_specs=[vmem, vmem, hbm, hbm, hbm],
        out_specs=vmem,
        scratch_shapes=[
            pltpu.VMEM((sections, positions, columns), bf16),
            pltpu.VMEM((sections, positions, columns), bf16),
            pltpu.VMEM((3, sections, depth, columns), bf16),
            pltpu.VMEM(rows, bf16),
            pltpu.VMEM(rows, bf16),
            pltpu.VMEM(moving, bf16),
            pltpu.VMEM(moving, bf16),
            pltpu.VMEM(moving, bf16),
            pltpu.VMEM(chains, bf16),
            pltpu.VMEM(chains, bf16),
            pltpu.VMEM(chains, bf16),
            dma((3,)),
            dma((3, sections)),
            dma((3, sections)),
            dma((blocks,)),
            dma((planes,)),
            dma((2, planes, tensors)),
            dma((2, planes, sections)),
            dma((blocks, planes)),
            dma((blocks, planes)),
            dma((blocks, planes)),
            dma(chains[:3]),
            dma(chains[:3]),
            dma(chains[:3]),
            dma((2, sections)),
            dma((2, sections)),
        ],
        compiler_params=pltpu.CompilerParams(
            collective_id=0, has_side_effects=True, vmem_limit_bytes=56 * 2**20
        ),
        cost_estimate=pl.CostEstimate(
            flops=6 * planes * positions * sections * depth * columns,
            bytes_accessed=2 * (picks.size + 3 * w_key.size),
            transcendentals=0,
        ),
    )(enc, picks, w_key, w_value, w_query)


def make(mesh):
    def on_device(target_ids, embed_table, encoder_out, w_query, w_key, w_value):
        table_rows = embed_table.shape[0]
        offset_ids = target_ids - lax.axis_index("dp") * table_rows
        inside = (offset_ids >= 0) & (offset_ids < table_rows)
        picked = jnp.take(
            embed_table, jnp.where(inside, offset_ids, table_rows), axis=0, mode="fill", fill_value=0
        )
        return projections(mesh, encoder_out[0], picked, w_key, w_value, w_query)[None]

    return on_device


def solution(mesh):
    in_specs = (
        P(None, "section"),
        P("dp", "tensor"),
        P("dp", "section", "tensor"),
        P(("section", "dp"), "tensor"),
        P(("section", "dp"), "tensor"),
        P(("section", "dp"), "tensor"),
    )
    out_specs = P("dp", "section", "tensor")
    return jax.shard_map(
        make(mesh), mesh=mesh, in_specs=in_specs, out_specs=out_specs, check_vma=False
    )
```

time: 210 us -> 199 us (0.948)
  the two profiles are of different devices: /device:TPU:9 before, /device:TPU:12 now
where the time goes in v3:
time: 199 us
  Pallas kernels  181 us (91%)
  local copies, waits for them, and re-layouts  14.6 us (7%)
  other arithmetic  2.97 us (1%)
    pallas_call x1, Pallas kernels, projections(): pl.pallas_call(functools.partial(project_kernel, sections, tensors, plane...  181 us
    gather x1, local copies, waits for them, and re-layouts, on_device(): jnp.take(embed_table, jnp.where(inside, offset_ids, table_rows), axis=0,...  12.8 us

profile of v3, /device:TPU:12, one launch (start us, length us, event | category | flops | bytes accessed | tf_op | source)
XLA Modules:
  0.0 198.5 jit_solution(16854256326813381498)
XLA Ops:
  0.0 0.7 compare_and_fusion
  0.7 0.7 fusion
  1.4 12.8 %gather_fusion = bf16[1024,1024]{1,0:T(8,128)(2,1)S(1)} fusion(bf16[8032,1024]{1,0:T(8,128)(2,1)} %param.7, s32[1024]{0:T(1024)S(1)} %broadcast_clamp_fusion), kind=kCustom, calls=%fused_computation | custom fusion | bytes 4198400 | tf_op jit(solution)/shard_map/jit(_take)/gather | solution.py:341
  14.2 1.6 broadcast_select_fusion.picks
  15.8 180.9 %shard_map.64 = bf16[256,1024]{1,0:T(8,128)(2,1)} custom-call(bf16[256,1024]{1,0:T(8,128)(2,1)} %bitcast.9, bf16[4,256,1024]{2,1,0:T(8,128)(2,1)} %broadcast_select_fusion.picks, bf16[512,1024]{1,0:T(8,128)(2,1)} %w_key.1, bf16[512,1024]{1,0:T(8,128)(2,1)} %w_value.1, bf16[512,1024]{1,0:T(8,128)(2,1)} %w_query.1), custom_call_target="tpu_custom_call" | custom-call | flops 6442450944 | bytes 5242880 | tf_op jit(solution)/shard_map/pallas_call | solution.py:292
  196.6 1.9 copy.9
  (2 shorter events, 0.0 us)

commit v4 on v3

--- a/solution.py
+++ b/solution.py
@@ -16,9 +16,9 @@
     sections, tensors, planes,
     enc, picks, w_key, w_value, w_query,
     out,
-    k_all, v_all, wbuf, x_enc, x_dec, rs_up, rs_dn, rs_out, sums, up, dn,
+    k_all, v_all, wbuf, x_enc, x_dec, rs_up, rs_dn, rs_out, sums, held_sums,
     w_local, w_send, w_recv, z_send, z_recv, e_send, e_recv,
-    r_send, r_up, r_dn, c_send, c_up, c_dn, o_send, o_recv,
+    r_send, r_up, r_dn, c_send, c_recv, o_send, o_recv,
 ):
     s, t, d = lax.axis_index("section"), lax.axis_index("tensor"), lax.axis_index("dp")
     depth, columns = w_key.shape
@@ -96,13 +96,13 @@
         def _():
             x_enc[d, rank] = enc[:, pl.ds(i * depth, depth)]
 
-    def clear(ref):
-        @pl.loop(0, 3 * planes)
+    def clear(way):
+        @pl.loop(0, 3 * chunks)
         def _(n):
-            ref[n // planes, lax.rem(n, planes)] = jnp.zeros(ref.shape[2:], ref.dtype)
-
-    pl.when(d == 0)(lambda: clear(up))
-    pl.when(d == planes - 1)(lambda: clear(dn))
+            held_sums[way, n // chunks, d, lax.rem(n, chunks)] = jnp.zeros((enc.shape[0], HD), enc.dtype)
+
+    pl.when(d == 0)(lambda: clear(0))
+    pl.when(d == planes - 1)(lambda: clear(1))
 
     def spread(kind, buffer):
         for b in sorted(range(planes), key=lambda b: (min(b, planes - 1 - b), -b)):
@@ -167,37 +167,42 @@
         return total
 
     def chain(j, x, gate):
+        near = jnp.where(d < planes // 2, 0, 1)
         for step in range(planes - 1):
-            for b, to, held, sem, has in (
-                (planes - 1 - step, 1, up, c_up, d > 0),
-                (step, planes - 1, dn, c_dn, d < planes - 1),
-            ):
-
-                @pl.when(gate & (b > d if to == 1 else b < d))
+            for way in (near, 1 - near):
+                rising = way == 0
+                b = jnp.where(rising, planes - 1 - step, step)
+                has = jnp.where(rising, d, planes - 1 - d) > 0
+                to = lax.rem(d + jnp.where(rising, 1, planes - 1), planes)
+
+                @pl.when(gate & (jnp.where(rising, b - d, d - b) > 0))
                 def _():
                     @pl.loop(0, chunks)
                     def _(n):
+                        total = product(j, x, b, n)
+
                         @pl.when(has)
                         def _():
-                            received(held.at[j, b, n], sem.at[j, b, n])
-
-                        total = product(j, x, b, n) + held[j, b, n].astype(jnp.float32)
-                        sums[j, b, n] = total.astype(jnp.bfloat16)
-                        remote(sums.at[j, b, n], held.at[j, b, n], c_send.at[j, b, n], sem.at[j, b, n],
-                               dp=lax.rem(d + to, planes)).start()
+                            received(held_sums.at[way, j, b, n], c_recv.at[way, j, b, n])
+                            rest = held_sums[way, j, b, n].astype(jnp.float32)
+                            sums[j, b, n] = (total + rest).astype(jnp.bfloat16)
+
+                        @pl.when(jnp.logical_not(has))
+                        def _():
+                            sums[j, b, n] = total.astype(jnp.bfloat16)
+
+                        remote(sums.at[j, b, n], held_sums.at[way, j, b, n], c_send.at[j, b, n],
+                               c_recv.at[way, j, b, n], dp=to).start()
 
     def whole(j, x, n):
         total = product(j, x, d, n)
-
-        @pl.when(d > 0)
-        def _():
-            received(up.at[j, d, n], c_up.at[j, d, n])
-
-        @pl.when(d < planes - 1)
-        def _():
-            received(dn.at[j, d, n], c_dn.at[j, d, n])
-
-        rest = up[j, d, n].astype(jnp.float32) + dn[j, d, n].astype(jnp.float32)
+        for way, has in ((0, d > 0), (1, d < planes - 1)):
+
+            @pl.when(has)
+            def _():
+                received(held_sums.at[way, j, d, n], c_recv.at[way, j, d, n])
+
+        rest = held_sums[0, j, d, n].astype(jnp.float32) + held_sums[1, j, d, n].astype(jnp.float32)
         return (total + rest).astype(jnp.bfloat16)
 
     def finish(j, x, result):
@@ -224,9 +229,9 @@
             )
             out[:, cols] = (total / weight_sum).astype(jnp.bfloat16)
 
-    def share(j, result):
+    def share(j, result, gate):
         for shift in range(1, sections):
-            send(always, result.at[s], result.at[s], o_send.at[j, shift], o_recv.at[j, s],
+            send(gate, result.at[s], result.at[s], o_send.at[j, shift], o_recv.at[j, s],
                  section=lax.rem(s + shift, sections))
 
     spread(ENCODER, x_enc)
@@ -251,14 +256,22 @@
     have_weight(VALUE)
     start_weight(QUERY, w_query)
     chain(VALUE, x_enc, always)
-    finish(KEY, x_enc, k_all.at[s])
-    share(KEY, k_all)
+
+    def keys_done(gate):
+        @pl.when(gate)
+        def _():
+            finish(KEY, x_enc, k_all.at[s])
+
+        share(KEY, k_all, gate)
+
+    keys_done(jnp.logical_not(edge))
     for b in range(planes):
         have_spread(DECODER, x_dec, b)
     have_weight(QUERY)
     chain(QUERY, x_dec, always)
+    keys_done(edge)
     finish(VALUE, x_enc, v_all.at[s])
-    share(VALUE, v_all)
+    share(VALUE, v_all, always)
     for j, result in ((KEY, k_all), (VALUE, v_all)):
         for shift in range(1, sections):
             other = lax.rem(s + shift, sections)
@@ -273,7 +286,7 @@
             def _():
                 @pl.loop(0, chunks)
                 def _(n):
-                    remote(sums.at[j, b, n], sums.at[j, b, n], c_send.at[j, b, n], c_up.at[j, b, n],
+                    remote(sums.at[j, b, n], sums.at[j, b, n], c_send.at[j, b, n], c_recv.at[0, j, b, n],
                            dp=lax.rem(d + 1, planes)).wait_send()
 
 
@@ -304,8 +317,7 @@
             pltpu.VMEM(moving, bf16),
             pltpu.VMEM(moving, bf16),
             pltpu.VMEM(chains, bf16),
-            pltpu.VMEM(chains, bf16),
-            pltpu.VMEM(chains, bf16),
+            pltpu.VMEM((2,) + chains, bf16),
             dma((3,)),
             dma((3, sections)),
             dma((3, sections)),
@@ -317,8 +329,7 @@
             dma((blocks, planes)),
             dma((blocks, planes)),
             dma(chains[:3]),
-            dma(chains[:3]),
-            dma(chains[:3]),
+            dma((2,) + chains[:3]),
             dma((2, sections)),
             dma((2, sections)),
         ],

time: 199 us -> 184 us (0.925); the launches traced: 199 us -> 180 us
  Pallas kernels: 181 us -> 163 us
    pallas_call x1, Pallas kernels: 181 us -> 163 us  [projections(): pl.pallas_call(functools.partial(project_kernel, sections, tensors, plane...]
where the time goes in v4:
time: 184 us; the launch traced here: 180 us
  Pallas kernels  163 us (89%)
  local copies, waits for them, and re-layouts  14.6 us (8%)
  other arithmetic  2.97 us (2%)
    pallas_call x1, Pallas kernels, projections(): pl.pallas_call(functools.partial(project_kernel, sections, tensors, plane...  163 us
    gather x1, local copies, waits for them, and re-layouts, on_device(): jnp.take(embed_table, jnp.where(inside, offset_ids, table_rows), axis=0,...  12.8 us

profile of v4, /device:TPU:12, one launch (start us, length us, event | category | flops | bytes accessed | tf_op | source)
XLA Modules:
  0.0 180.4 jit_solution(5513802731492567945)
XLA Ops:
  0.0 0.7 compare_and_fusion
  0.7 0.7 fusion
  1.4 12.8 %gather_fusion = bf16[1024,1024]{1,0:T(8,128)(2,1)S(1)} fusion(bf16[8032,1024]{1,0:T(8,128)(2,1)} %param.7, s32[1024]{0:T(1024)S(1)} %broadcast_clamp_fusion), kind=kCustom, calls=%fused_computation | custom fusion | bytes 4198400 | tf_op jit(solution)/shard_map/jit(_take)/gather | solution.py:352
  14.2 1.6 broadcast_select_fusion.picks
  15.8 162.8 %shard_map.64 = bf16[256,1024]{1,0:T(8,128)(2,1)} custom-call(bf16[256,1024]{1,0:T(8,128)(2,1)} %bitcast.9, bf16[4,256,1024]{2,1,0:T(8,128)(2,1)} %broadcast_select_fusion.picks, bf16[512,1024]{1,0:T(8,128)(2,1)} %w_key.1, bf16[512,1024]{1,0:T(8,128)(2,1)} %w_value.1, bf16[512,1024]{1,0:T(8,128)(2,1)} %w_query.1), custom_call_target="tpu_custom_call" | custom-call | flops 6442450944 | bytes 5242880 | tf_op jit(solution)/shard_map/pallas_call | solution.py:305
  178.5 1.9 %copy.9 = bf16[1,256,1024]{2,1,0:T(8,128)(2,1)} copy(bf16[1,256,1024]{2,1,0:T(8,128)(2,1)} %bitcast.7) | data formatting | bytes 1048576
  (2 shorter events, 0.0 us)

commit v5 on v4

--- a/solution.py
+++ b/solution.py
@@ -257,21 +257,21 @@
     start_weight(QUERY, w_query)
     chain(VALUE, x_enc, always)
 
-    def keys_done(gate):
-        @pl.when(gate)
-        def _():
-            finish(KEY, x_enc, k_all.at[s])
-
-        share(KEY, k_all, gate)
-
-    keys_done(jnp.logical_not(edge))
+    def memory_done(gate):
+        for j, result in ((KEY, k_all), (VALUE, v_all)):
+
+            @pl.when(gate)
+            def _():
+                finish(j, x_enc, result.at[s])
+
+            share(j, result, gate)
+
+    memory_done(jnp.logical_not(edge))
     for b in range(planes):
         have_spread(DECODER, x_dec, b)
     have_weight(QUERY)
     chain(QUERY, x_dec, always)
-    keys_done(edge)
-    finish(VALUE, x_enc, v_all.at[s])
-    share(VALUE, v_all, always)
+    memory_done(edge)
     for j, result in ((KEY, k_all), (VALUE, v_all)):
         for shift in range(1, sections):
             other = lax.rem(s + shift, sections)

time: 184 us -> 176 us (0.957)
  Pallas kernels: 163 us -> 156 us
    pallas_call x1, Pallas kernels: 163 us -> 156 us  [projections(): pl.pallas_call(functools.partial(project_kernel, sections, tensors, plane...]
where the time goes in v5:
time: 176 us; the launch traced here: 173 us
  Pallas kernels  156 us (89%)
  local copies, waits for them, and re-layouts  14.6 us (8%)
  other arithmetic  2.97 us (2%)
    pallas_call x1, Pallas kernels, projections(): pl.pallas_call(functools.partial(project_kernel, sections, tensors, plane...  156 us
    gather x1, local copies, waits for them, and re-layouts, on_device(): jnp.take(embed_table, jnp.where(inside, offset_ids, table_rows), axis=0,...  12.8 us

profile of v5, /device:TPU:12, one launch (start us, length us, event | category | flops | bytes accessed | tf_op | source)
XLA Modules:
  0.0 173.2 jit_solution(5184204593618894116)
XLA Ops:
  0.0 0.7 compare_and_fusion
  0.7 0.7 fusion
  1.4 12.8 %gather_fusion = bf16[1024,1024]{1,0:T(8,128)(2,1)S(1)} fusion(bf16[8032,1024]{1,0:T(8,128)(2,1)} %param.7, s32[1024]{0:T(1024)S(1)} %broadcast_clamp_fusion), kind=kCustom, calls=%fused_computation | custom fusion | bytes 4198400 | tf_op jit(solution)/shard_map/jit(_take)/gather | solution.py:352
  14.2 1.6 broadcast_select_fusion.picks
  15.8 155.6 %shard_map.64 = bf16[256,1024]{1,0:T(8,128)(2,1)} custom-call(bf16[256,1024]{1,0:T(8,128)(2,1)} %bitcast.9, bf16[4,256,1024]{2,1,0:T(8,128)(2,1)} %broadcast_select_fusion.picks, bf16[512,1024]{1,0:T(8,128)(2,1)} %w_key.1, bf16[512,1024]{1,0:T(8,128)(2,1)} %w_value.1, bf16[512,1024]{1,0:T(8,128)(2,1)} %w_query.1), custom_call_target="tpu_custom_call" | custom-call | flops 6442450944 | bytes 5242880 | tf_op jit(solution)/shard_map/pallas_call | solution.py:305
  171.4 1.9 %copy.9 = bf16[1,256,1024]{2,1,0:T(8,128)(2,1)} copy(bf16[1,256,1024]{2,1,0:T(8,128)(2,1)} %bitcast.7) | data formatting | bytes 1048576
  (2 shorter events, 0.0 us)
